TPU v7x, 32 devices: a whole 2x2x4 slice. The times are simulated.
32 devices in a mesh: vocab: 4 (over z), prange: 4 (over y, x), query: 2 (over core).
Axes of the slice: x: 2, y: 2, z: 4, core: 2. Of those that a mesh axis runs over, the one named last changes fastest.
Arguments:
- term_ids: int32 [4096, 32], P('query'), may hold values from 0 to 32767
- term_weights: bfloat16 [4096, 32], P('query'), may hold values from 0.049804688 to 1
- impact: bfloat16 [32768, 8192], P('vocab', 'prange'), may hold values from 0.0099487305 to 1
- query_rows: bfloat16 [128, 32768], P(('prange', 'query'), 'vocab'), may hold values from -0.3125 to 0.3125
- candidates: int32 [128, 4], P(('prange', 'query')), may hold values from 0 to 63, all different within a row; in each aligned block of 16 rows (0 to 15, 16 to 31, ...) at most 2 rows name the same one
Outputs:
- first_scores: bfloat16 [4, 2048, 4096], P('prange', 'vocab', 'query')
- rescored: float32 [128, 4, 128], P(('prange', 'query'), None, 'vocab')
Inputs may be any that keep to these rules, and one draw needn't show every extreme that they name: `candidates`: each row names 4 different blocks. The 16 rows held by one device name any block at most 2 times, and some block exactly 2 times.
All inputs are finite; a program needn't handle non-finite values.
Results may differ from a plain program's by a relative error of at most 0.019.
Values may be sent and summed in bfloat16 or wider, within the bound.
A program may use at most 192 MiB of HBM per device.

v0:
```python
import jax
import jax.numpy as jnp
from jax import lax
from jax.sharding import PartitionSpec as P

BLOCK = 128
CANDS = 4
MOST = 2


def local(term_ids, term_weights, impact, query_rows, candidates):
    shard_width = impact.shape[0]
    query_count = term_ids.shape[0]
    term_count = term_ids.shape[1]
    shard_index = lax.axis_index("vocab")
    local_ids = term_ids - shard_index * shard_width
    columns_here = jnp.arange(shard_width, dtype=jnp.int32)[None, :]
    weights_wide = term_weights.astype(jnp.float32)
    dense_sum = jnp.zeros((query_count, shard_width), jnp.float32)
    for slot in range(term_count):
        dense_sum = dense_sum + jnp.where(
            local_ids[:, slot : slot + 1] == columns_here, weights_wide[:, slot : slot + 1], 0.0
        )
    dense_query = dense_sum.astype(jnp.bfloat16)
    first_scores = lax.psum_scatter(
        lax.dot_general(
            impact, dense_query, (((0,), (1,)), ((), ())), preferred_element_type=jnp.float32
        ).astype(jnp.bfloat16),
        "vocab",
        scatter_dimension=0,
        tiled=True,
    )[None]
    range_count = lax.axis_size("prange")
    resident_blocks = impact.shape[1] // BLOCK
    slot_count = range_count * resident_blocks * MOST
    full_count = query_rows.shape[0]
    flat_blocks = candidates.reshape(-1)
    pair_count = flat_blocks.shape[0]
    pair_order = jnp.arange(pair_count, dtype=jnp.int32)
    same_block = flat_blocks[:, None] == flat_blocks[None, :]
    earlier = pair_order[None, :] < pair_order[:, None]
    pair_rank = jnp.sum((same_block & earlier).astype(jnp.int32), axis=1)
    slot_index = flat_blocks * MOST + pair_rank
    placed = (slot_index[None, :] == jnp.arange(slot_count, dtype=jnp.int32)[:, None]).astype(
        jnp.float32
    )
    owner_rows = (
        (pair_order // CANDS)[:, None] == jnp.arange(full_count, dtype=jnp.int32)[None, :]
    ).astype(jnp.float32)
    picker = jnp.dot(placed, owner_rows, precision=lax.Precision.HIGHEST).astype(jnp.bfloat16)
    outgoing = jnp.dot(picker, query_rows, preferred_element_type=jnp.float32).astype(jnp.bfloat16)
    outgoing = outgoing.reshape(range_count, resident_blocks, MOST, shard_width)
    arrived = lax.all_to_all(outgoing, "prange", split_axis=0, concat_axis=0, tiled=True)
    block_tiles = impact.reshape(shard_width, resident_blocks, BLOCK)
    partial_score_value = jnp.einsum(
        "sbmv,vbp->sbmp", arrived, block_tiles, preferred_element_type=jnp.float32
    )
    reduced = lax.psum_scatter(
        partial_score_value.astype(jnp.bfloat16), "vocab", scatter_dimension=3, tiled=True
    ).astype(jnp.float32)
    returned = lax.all_to_all(reduced, "prange", split_axis=0, concat_axis=0, tiled=True).reshape(
        slot_count, -1
    )
    paired = lax.dot_general(
        placed,
        returned,
        (((0,), (0,)), ((), ())),
        precision=lax.Precision.HIGHEST,
        preferred_element_type=jnp.float32,
    )
    rescored = paired.reshape(full_count, CANDS, -1)
    return (first_scores, rescored)


def solution(mesh):
    return jax.shard_map(
        local,
        mesh=mesh,
        in_specs=(
            P("query", None),
            P("query", None),
            P("vocab", "prange"),
            P(("prange", "query"), "vocab"),
            P(("prange", "query"), None),
        ),
        out_specs=(P("prange", "vocab", "query"), P(("prange", "query"), None, "vocab")),
        check_vma=False,
    )
```

profile of v0, /device:TPU:0, one launch (start us, length us, event | category | flops | bytes accessed | tf_op | source)
XLA Modules:
  0.0 775.0 jit_solution(13683952017290665715)
XLA Ops:
  7.2 0.0 copy-start
  7.2 0.8 copy.42
  8.0 0.1 reshape.58
  8.1 0.2 convert_reduce_fusion
  8.3 0.0 copy-start.3
  8.3 0.5 copy-done.3
  8.8 0.2 convolution_convert_fusion.1
  9.0 0.0 copy-done
  9.0 0.7 convolution_convert_fusion
  9.8 2.6 reshape.59
  12.4 5.2 all-to-all-start
  17.6 0.0 reduce-scatter.7.cloned.1.call-start
  17.6 1.0 broadcast_subtract_fusion
  18.5 0.1 fusion.87
  18.7 0.1 fusion.88
  18.7 1.4 fusion.89
  20.1 1.2 fusion.90
  21.3 460.2 %add_convert_fusion.6 = bf16[2048,8192]{1,0:T(8,128)(2,1)} fusion(f32[2048]{0:T(1024)S(1)} %bitcast.158, s32[2048]{0:T(1024)S(1)} %bitcast.96, f32[2048]{0:T(1024)S(1)} %bitcast.157, s32[2048]{0:T(1024)S(1)} %bitcast.97, f32[2048]{0:T(1024)S(1)} %bitcast.156, s32[2048]{0:T(1024)S(1)} %bitcast.98, f32[2048]{0:T(1024)S(1)} %bitcast.155, ...), kind=kLoop, calls=%fused_computation.clone.clone.clone.clone.1 | loop fusion | flops 1610612736 | bytes 34078720 | tf_op jit(solution)/shard_map/dot_general | solution.py:26
  481.5 23.1 %copy.61 = bf16[1024,8,16,128]{3,2,1,0:T(8,128)(2,1)} copy(bf16[1024,8,16,128]{3,1,2,0:T(8,128)(2,1)} %bitcast.89) | data formatting | bytes 67108864
  504.6 0.0 all-to-all-done
  504.6 30.3 %fusion.74 = bf16[4,16,2,128]{3,2,0,1:T(2,128)(2,1)S(1)} fusion(bf16[8192,16,128,1]{2,1,0,3:T(8,128)(2,1)} %bitcast.90, bf16[4,16,2,8192]{3,2,1,0:T(2,128)(2,1)S(1)} %all-to-all-done), kind=kOutput, calls=%fused_computation.105 | convolution fusion | flops 268451840 | bytes 35684352 | tf_op jit(solution)/shard_map/sbmv,vbp->sbmp/dot_general | solution.py:55
  534.9 1.1 copy.57
  536.0 2.5 reshape.64
  538.5 0.0 reduce-scatter.7.cloned.1.call-update
  538.5 0.0 copy-start.4
  538.6 0.0 copy-start.2
  538.6 0.0 reduce-scatter.5.cloned.1.call-start
  538.6 0.0 copy-start.1
  538.6 79.3 %convert_bitcast_fusion = bf16[2048,2048]{0,1:T(8,128)(2,1)} fusion(bf16[8192,2048]{1,0:T(8,128)(2,1)} %param.7, bf16[2048,8192]{1,0:T(8,128)(2,1)} %add_convert_fusion.6), kind=kOutput, calls=%fused_computation.102 | convolution fusion | flops 68723671040 | bytes 75497472 | tf_op jit(solution)/shard_map/dot_general | solution.py:26
  617.9 0.0 reduce-scatter.5.cloned.1.call-update
  617.9 0.0 copy-done.4
  617.9 0.1 reduce_sum.12
  618.0 0.1 copy.43
  618.1 0.0 reduce-scatter.7.cloned.1.call-done
  618.1 1.3 reshape.65
  619.4 0.4 copy.47
  619.8 0.7 reshape.66
  620.5 4.2 all-to-all-start.1
  624.7 0.0 copy-done.2
  624.7 4.7 all-to-all-done.1
  629.4 0.5 broadcast.46
  629.9 0.7 reduce
  630.6 0.1 reshape.67
  630.7 0.2 fusion.82
  631.0 0.6 copy.51
  631.6 132.7 %reduce-scatter.5.cloned.1.call-done = bf16[512,2048]{0,1:T(8,128)(2,1)} async-done(((bf16[2048,2048]{0,1:T(8,128)(2,1)}), bf16[512,2048]{0,1:T(8,128)(2,1)}) %reduce-scatter.5.cloned.1.call-update) | async-done | bytes 2097168 | tf_op jit(solution)/shard_map/reduce_scatter | solution.py:25
  764.3 3.9 copy.50
  768.2 0.0 copy-done.1
  (3 shorter events, 0.0 us)
Async XLA Ops:
  7.2 1.9 copy-start
  8.3 0.5 copy-start.3
  12.4 492.2 %all-to-all-start = ((bf16[4,16,2,8192]{3,2,1,0:T(2,128)(2,1)}), bf16[4,16,2,8192]{3,2,1,0:T(2,128)(2,1)S(1)}, u32[]{:S(2)}, u32[]{:S(2)}) async-start(bf16[4,16,2,8192]{3,2,1,0:T(2,128)(2,1)} %reshape.59), calls=%async_computation.1 | async-start | bytes 4194304 | tf_op jit(solution)/shard_map/all_to_all | solution.py:53
  17.6 600.5 %reduce-scatter.7.cloned.1.call-start = ((), (), s32[]{:S(2)}) async-start(), calls=%async_computation.5 | async-start | bytes 40960
  538.5 79.4 %copy-start.4 = (s32[64]{0:T(128)S(1)}, s32[64]{0:T(128)}, u32[]{:S(2)}) copy-start(s32[64]{0:T(128)} %copy-done.3) | copy-start | bytes 772
  538.6 86.1 %copy-start.2 = (s32[16,4]{0,1:T(4,128)S(1)}, s32[16,4]{0,1:T(4,128)}, u32[]{:S(2)}) copy-start(s32[16,4]{0,1:T(4,128)} %param.9) | copy-start | bytes 772
  538.6 225.7 %reduce-scatter.5.cloned.1.call-start = ((), (), s32[]{:S(2)}) async-start(), calls=%async_computation.4 | async-start | bytes 10485760 | tf_op jit(solution)/shard_map/reduce_scatter | solution.py:25
  538.6 229.6 %copy-start.1 = (bf16[16,8192]{1,0:T(8,128)(2,1)S(1)}, bf16[16,8192]{1,0:T(8,128)(2,1)}, u32[]{:S(2)}) copy-start(bf16[16,8192]{1,0:T(8,128)(2,1)} %param.8) | copy-start | bytes 786436
  620.5 8.9 %all-to-all-start.1 = ((f32[4,1,1024]{2,1,0:T(1,128)}), f32[4,1,1024]{2,1,0:T(1,128)S(1)}, u32[]{:S(2)}, u32[]{:S(2)}) async-start(f32[4,1,1024]{2,1,0:T(1,128)} %reshape.66), calls=%async_computation.2 | async-start | bytes 32768 | tf_op jit(solution)/shard_map/all_to_all | solution.py:61
Sparse Core Ops, SparseCore 0:
  538.7 20.6 reduce-scatter.6
  618.0 146.1 reduce-scatter.4
where the time goes:
time: 776 us; the launch traced here: 775 us
  other arithmetic  462 us (60%)
  waiting for transfers between devices  137 us (18%)
  matrix products  111 us (14%)
  local copies, waits for them, and re-layouts  41.2 us (5%)
  between operations  14.2 us (2%)
  starting transfers between devices  9.41 us (1%)
    dot_general x1, other arithmetic, local(): lax.dot_general(impact, dense_query, (((0,), (1,)), ((), ())), preferred_...  460 us
    reduce_scatter x1, waiting for transfers between devices, local(): lax.psum_scatter(lax.dot_general(impact, dense_query, (((0,), (1,)), ((),...  133 us
    dot_general x1, matrix products, local(): lax.dot_general(impact, dense_query, (((0,), (1,)), ((), ())), preferred_...  79.3 us
    unnamed x19, local copies, waits for them, and re-layouts  34.7 us
    dot_general x1, matrix products, local(): jnp.einsum('sbmv,vbp->sbmp', arrived, block_tiles, preferred_element_type...  30.3 us
  transfers between devices with their start and end apart: 4, of which 2 were waited for; matrix products, arithmetic and copies ran while one was open for 74% of the time, Pallas kernels for 0%

commit v1 on v0

v1 whole, which is shorter than its diff:
```python
import functools

import jax
import jax.numpy as jnp
from jax import lax
from jax.experimental import pallas as pl
from jax.experimental.pallas import tpu as pltpu
from jax.sharding import PartitionSpec as P

BLOCK = 128
LOW = 256
GROUP = 8
CHUNKS = (2, 2, 4, 4, 4)


def dense_kernel(high_count, high_ref, low_ref, weight_ref, dense_ref):
    columns = high_ref.shape[1]
    rows = high_count * GROUP
    row_codes = lax.broadcasted_iota(jnp.int32, (rows, columns), 0).astype(jnp.float32).astype(jnp.bfloat16)
    low_codes = lax.broadcasted_iota(jnp.int32, (LOW, columns), 0).astype(jnp.float32).astype(jnp.bfloat16)
    zero = jnp.zeros((), jnp.bfloat16)
    one = jnp.ones((), jnp.bfloat16)

    def group_product(g):
        high = high_ref[g : g + 1, :].astype(jnp.bfloat16)
        low = low_ref[g : g + 1, :].astype(jnp.bfloat16)
        weight = weight_ref[g : g + 1, :].astype(jnp.bfloat16)
        weighted = jnp.where(row_codes == high, jnp.broadcast_to(weight, row_codes.shape), zero)
        picked = jnp.where(low_codes == low, one, zero)
        product = lax.dot_general(
            weighted, picked, (((1,), (1,)), ((), ())), preferred_element_type=jnp.float32
        )
        return product.reshape(high_count, GROUP, LOW)

    for pair in range(high_ref.shape[0] // 2):
        both = jnp.concatenate(
            [group_product(2 * pair), group_product(2 * pair + 1)], axis=1
        ).astype(jnp.bfloat16)
        for h in range(high_count):
            dense_ref[pair * 2 * GROUP : (pair + 1) * 2 * GROUP, h * LOW : (h + 1) * LOW] = both[h]


def densify(high, low, weight, shard_width):
    groups, columns = high.shape
    high_count = shard_width // LOW
    step = 8
    spec = pl.BlockSpec((step, columns), lambda i: (i, 0))
    return pl.pallas_call(
        functools.partial(dense_kernel, high_count),
        grid=(groups // step,),
        in_specs=[spec] * 3,
        out_specs=pl.BlockSpec((step * GROUP, shard_width), lambda i: (i, 0)),
        out_shape=jax.ShapeDtypeStruct((groups * GROUP, shard_width), jnp.bfloat16),
        compiler_params=pltpu.CompilerParams(vmem_limit_bytes=24 * 1024 * 1024),
        cost_estimate=pl.CostEstimate(
            flops=2 * groups * columns * LOW * high_count * GROUP,
            bytes_accessed=2 * groups * GROUP * shard_width,
            transcendentals=0,
        ),
    )(high, low, weight)


def local(term_ids, term_weights, impact, query_rows, candidates):
    shard_width, range_width = impact.shape
    query_count, term_count = term_ids.shape
    range_count = lax.axis_size("prange")
    vocab_count = lax.axis_size("vocab")
    resident_blocks = range_width // BLOCK
    high_count = shard_width // LOW

    all_rows = lax.all_gather(query_rows, "prange", axis=0, tiled=True)
    all_candidates = lax.all_gather(candidates, "prange", axis=0, tiled=True)

    local_ids = term_ids - lax.axis_index("vocab") * shard_width
    high = local_ids // LOW
    low = (local_ids % LOW).astype(jnp.float32)
    lane = jnp.arange(query_count, dtype=jnp.int32)[:, None] % GROUP
    high_code = jnp.where((high >= 0) & (high < high_count), high * GROUP + lane, -1)
    group_shape = (query_count // GROUP, GROUP * term_count)
    high_code = high_code.astype(jnp.float32).reshape(group_shape)
    low = low.reshape(group_shape)
    weight = term_weights.astype(jnp.float32).reshape(group_shape)

    pieces = []
    begin = 0
    codes = (high_code, low, weight)
    for share in CHUNKS:
        size = group_shape[0] * share // sum(CHUNKS)
        cut = slice(begin, begin + size)
        begin += size
        dense_query = densify(*(code[cut] for code in codes), shard_width)
        part = lax.dot_general(
            impact, dense_query, (((0,), (1,)), ((), ())), preferred_element_type=jnp.float32
        ).astype(jnp.bfloat16)
        codes, all_rows, part = lax.optimization_barrier((codes, all_rows, part))
        pieces.append(lax.psum_scatter(part, "vocab", scatter_dimension=0, tiled=True))
        if len(pieces) >= 3:
            codes, pieces[-3] = lax.optimization_barrier((codes, pieces[-3]))
        if len(pieces) == 3:
            scores = jnp.dot(all_rows, impact, preferred_element_type=jnp.float32)
            scores = scores.reshape(-1, resident_blocks, BLOCK)
            own = all_candidates - lax.axis_index("prange") * resident_blocks
            chosen = own[:, :, None] == jnp.arange(resident_blocks, dtype=jnp.int32)
            picked = jnp.sum(
                jnp.where(chosen[:, :, :, None], scores[:, None, :, :], 0.0), axis=2
            )
            full_count, cands = candidates.shape
            share_width = BLOCK // vocab_count
            picked = picked.reshape(range_count, full_count * cands, vocab_count, share_width)
            picked = picked.transpose(2, 0, 1, 3).reshape(
                vocab_count * range_count, full_count * cands * share_width
            )
            codes, picked, pieces[0] = lax.optimization_barrier((codes, picked, pieces[0]))
            summed = lax.psum_scatter(
                picked, ("vocab", "prange"), scatter_dimension=0, tiled=True
            )
            rescored = summed.reshape(full_count, cands, share_width)
    first_scores = jnp.concatenate(pieces, axis=1)[None]
    return (first_scores, rescored)


def solution(mesh):
    return jax.shard_map(
        local,
        mesh=mesh,
        in_specs=(
            P("query", None),
            P("query", None),
            P("vocab", "prange"),
            P(("prange", "query"), "vocab"),
            P(("prange", "query"), None),
        ),
        out_specs=(P("prange", "vocab", "query"), P(("prange", "query"), None, "vocab")),
        check_vma=False,
    )
```

time: 776 us -> 370 us (0.48)
  other arithmetic: 462 us -> 2.26 us
  waiting for transfers between devices: 137 us -> 199 us
  local copies, waits for them, and re-layouts: 41.2 us -> 14 us
  Pallas kernels: 0 us -> 15.7 us
  blocking collectives: 0 us -> 9.52 us
  starting transfers between devices: 9.41 us -> 0.68 us
    dot_general x1 -> x0, other arithmetic: 460 us -> none  [local(): lax.dot_general(impact, dense_query, (((0,), (1,)), ((), ())), preferred_...]
    unnamed x3 -> x8, waiting for transfers between devices: 0.03 us -> 66.9 us
    unnamed x19 -> x22, local copies, waits for them, and re-layouts: 34.7 us -> 6.79 us
    dot_general x1 -> x5, matrix products: 79.3 us -> 99.8 us  [local(): lax.dot_general(impact, dense_query, (((0,), (1,)), ((), ())), preferred_...]
    dot_general x4 -> x1, matrix products: 31.5 us -> 13.8 us  [local(): scores = jnp.dot(all_rows, impact, preferred_element_type=jnp.float32)]
    pallas_call x0 -> x5, Pallas kernels: none -> 15.7 us  [densify(): pl.pallas_call(functools.partial(dense_kernel, high_count), grid=(groups...]
    all_gather x0 -> x1, blocking collectives: none -> 9.52 us  [local(): all_candidates = lax.all_gather(candidates, 'prange', axis=0, tiled=True)]
    all_to_all x2 -> x0, starting transfers between devices: 9.37 us -> none  [the longest x1 5.17 us: local(): lax.all_to_all(outgoing, 'prange', split_axis=0, concat_axis=0, tiled=True)]
  transfers between devices with their start and end apart: 4 -> 7, of which waited for: 2 -> 4; matrix products, arithmetic and copies ran while one was open for 74% -> 34% of each run, Pallas kernels for 0% -> 4%
where the time goes in v1:
time: 370 us; the launch traced here: 369 us
  waiting for transfers between devices  199 us (54%)
  matrix products  114 us (31%)
  Pallas kernels  15.7 us (4%)
  between operations  14.5 us (4%)
  local copies, waits for them, and re-layouts  14 us (4%)
  blocking collectives  9.52 us (3%)
    reduce_scatter x5, waiting for transfers between devices, local(): lax.psum_scatter(part, 'vocab', scatter_dimension=0, tiled=True)  132 us
    dot_general x5, matrix products, local(): lax.dot_general(impact, dense_query, (((0,), (1,)), ((), ())), preferred_...  99.8 us
    unnamed x8, waiting for transfers between devices  66.9 us
    pallas_call x5, Pallas kernels, densify(): pl.pallas_call(functools.partial(dense_kernel, high_count), grid=(groups...  15.7 us
    dot_general x1, matrix products, local(): scores = jnp.dot(all_rows, impact, preferred_element_type=jnp.float32)  13.8 us
    all_gather x1, blocking collectives, local(): all_candidates = lax.all_gather(candidates, 'prange', axis=0, tiled=True)  9.52 us
  transfers between devices with their start and end apart: 7, of which 4 were waited for; matrix products, arithmetic and copies ran while one was open for 34% of the time, Pallas kernels for 4%

profile of v1, /device:TPU:0, one launch (start us, length us, event | category | flops | bytes accessed | tf_op | source)
XLA Modules:
  0.0 369.4 jit_solution(3010254113981118559)
XLA Ops:
  7.2 0.0 copy-start.5
  7.2 0.0 all-gather.3.cloned.1.call-start
  7.2 0.7 all-gather.3.cloned.1.call-update
  7.9 0.0 reduce-scatter.6.cloned.1.call-start
  8.0 1.3 fusion.5
  9.2 0.3 copy.34
  9.6 0.3 copy.35
  9.9 0.7 slice.74
  10.7 1.1 copy.36
  11.8 0.0 copy-done.5
  11.8 9.5 %all-gather = s32[4,16,4]{1,2,0:T(4,128)S(1)} all-gather(s32[1,16,4]{1,2,0:T(4,128)S(1)} %bitcast.40), channel_id=1, replica_groups=mesh['vocab'=4,'prange'=4,'query'=2] {'prange'}, dimensions={0}, use_global_device_ids=true | all-gather | bytes 1280 | tf_op jit(solution)/shard_map/all_gather | solution.py:72
  21.3 0.1 copy.44
  21.4 0.1 iota_compare_fusion
  21.6 0.1 copy.39
  21.7 0.1 slice.59.weight_ref
  21.8 0.1 copy.37
  21.9 0.1 slice.55.high_ref
  22.0 0.1 copy.38
  22.0 0.1 slice.57.low_ref
  22.2 0.3 reshape.45
  22.5 0.3 reshape.46
  22.8 0.0 copy-start.1
  22.8 0.3 reshape.47
  23.1 2.0 shard_map.68
  25.1 16.4 %fusion.3 = bf16[2048,256]{0,1:T(8,128)(2,1)} fusion(bf16[256,8192]{1,0:T(8,128)(2,1)S(1)} %shard_map.68, bf16[8192,2048]{1,0:T(8,128)(2,1)} %param.7), kind=kOutput, calls=%fused_computation.8 | convolution fusion | flops 8590458880 | bytes 38797312 | tf_op jit(solution)/shard_map/dot_general | solution.py:92
  41.5 0.0 reduce-scatter.6.cloned.1.call-update
  41.6 0.2 reduce-scatter.8.cloned.1.call-start
  41.8 2.0 shard_map.69
  43.8 16.5 %fusion.4 = bf16[2048,256]{0,1:T(8,128)(2,1)} fusion(bf16[256,8192]{1,0:T(8,128)(2,1)S(1)} %shard_map.69, bf16[8192,2048]{1,0:T(8,128)(2,1)} %param.7), kind=kOutput, calls=%fused_computation.9 | convolution fusion | flops 8590458880 | bytes 38797312 | tf_op jit(solution)/shard_map/dot_general | solution.py:92
  60.3 0.0 copy-done.1
  60.3 3.9 %shard_map.70 = bf16[512,8192]{1,0:T(8,128)(2,1)S(1)} custom-call(f32[64,256]{1,0:T(8,128)S(1)} %slice.63.high_ref, f32[64,256]{1,0:T(8,128)S(1)} %slice.64.low_ref, f32[64,256]{1,0:T(8,128)S(1)} %slice.65.weight_ref), custom_call_target="tpu_custom_call" | custom-call | flops 2147483648 | bytes 8388608 | tf_op jit(solution)/shard_map/pallas_call | solution.py:48
  64.2 0.0 copy-start
  64.2 22.3 %fusion = bf16[2048,512]{0,1:T(8,128)(2,1)} fusion(bf16[512,8192]{1,0:T(8,128)(2,1)S(1)} %shard_map.70, bf16[8192,2048]{1,0:T(8,128)(2,1)} %param.7), kind=kOutput, calls=%fused_computation.3 | convolution fusion | flops 17180917760 | bytes 44040192 | tf_op jit(solution)/shard_map/dot_general | solution.py:92
  86.5 0.0 reduce-scatter.8.cloned.1.call-update
  86.5 0.0 all-reduce.3.cloned.1.call-start
  86.6 0.0 copy-done
  86.6 13.8 %convolution_bitcast_fusion = f32[8,8,16,128]{3,1,2,0:T(8,128)S(1)} fusion(bf16[64,8192]{1,0:T(8,128)(2,1)S(1)} %copy-done, bf16[8192,2048]{1,0:T(8,128)(2,1)} %param.7), kind=kOutput, calls=%fused_computation.11 | convolution fusion | flops 2147483648 | bytes 35127296 | tf_op jit(solution)/shard_map/dot_general | solution.py:100
  100.4 0.1 copy.46
  100.5 0.9 select_reduce_fusion
  101.4 0.3 reshape.48
  101.7 0.9 reshape.49
  102.6 0.0 all-reduce.3.cloned.1.call-update
  102.7 0.0 reduce-scatter.10.cloned.1.call-start
  102.7 0.5 reduce-scatter.10.cloned.1.call-update
  103.2 0.3 reduce-scatter.12.cloned.1.call-start
  103.6 3.9 %shard_map.71 = bf16[512,8192]{1,0:T(8,128)(2,1)S(1)} custom-call(f32[64,256]{1,0:T(8,128)S(1)} %slice.66.high_ref, f32[64,256]{1,0:T(8,128)S(1)} %slice.67.low_ref, f32[64,256]{1,0:T(8,128)S(1)} %slice.68.weight_ref), custom_call_target="tpu_custom_call" | custom-call | flops 2147483648 | bytes 8388608 | tf_op jit(solution)/shard_map/pallas_call | solution.py:48
  107.5 22.3 %fusion.1 = bf16[2048,512]{0,1:T(8,128)(2,1)} fusion(bf16[512,8192]{1,0:T(8,128)(2,1)S(1)} %shard_map.71, bf16[8192,2048]{1,0:T(8,128)(2,1)} %param.7), kind=kOutput, calls=%fused_computation.4 | convolution fusion | flops 17180917760 | bytes 44040192 | tf_op jit(solution)/shard_map/dot_general | solution.py:92
  129.8 0.0 reduce-scatter.12.cloned.1.call-update
  129.8 0.0 reduce-scatter.14.cloned.1.call-start
  129.9 3.9 %shard_map.72 = bf16[512,8192]{1,0:T(8,128)(2,1)S(1)} custom-call(f32[64,256]{1,0:T(8,128)S(1)} %slice.69.high_ref, f32[64,256]{1,0:T(8,128)S(1)} %slice.70.low_ref, f32[64,256]{1,0:T(8,128)S(1)} %slice.71.weight_ref), custom_call_target="tpu_custom_call" | custom-call | flops 2147483648 | bytes 8388608 | tf_op jit(solution)/shard_map/pallas_call | solution.py:48
  133.8 0.0 copy-start.6
  133.8 22.3 %fusion.2 = bf16[2048,512]{0,1:T(8,128)(2,1)} fusion(bf16[512,8192]{1,0:T(8,128)(2,1)S(1)} %shard_map.72, bf16[8192,2048]{1,0:T(8,128)(2,1)} %param.7), kind=kOutput, calls=%fused_computation.5 | convolution fusion | flops 17180917760 | bytes 44040192 | tf_op jit(solution)/shard_map/dot_general | solution.py:92
  156.1 0.0 reduce-scatter.14.cloned.1.call-update
  156.2 0.6 dynamic-slice
  156.8 65.6 %all-reduce.3.cloned.1.call-done = f32[16,2048]{1,0:T(8,128)} async-done(((f32[16,2048]{1,0:T(8,128)}), f32[16,2048]{1,0:T(8,128)}) %all-reduce.3.cloned.1.call-update) | async-done | bytes 131088
  222.5 1.5 dynamic-slice_reduce_fusion
  224.0 0.7 reshape.50
  224.7 43.4 %reduce-scatter.10.cloned.1.call-done = bf16[512,512]{0,1:T(8,128)(2,1)} async-done(((bf16[2048,512]{0,1:T(8,128)(2,1)}), bf16[512,512]{0,1:T(8,128)(2,1)}) %reduce-scatter.10.cloned.1.call-update) | async-done | bytes 524304 | tf_op jit(solution)/shard_map/reduce_scatter | solution.py:96
  268.1 1.1 constant_dynamic-update-slice_fusion.2
  269.2 44.4 %reduce-scatter.12.cloned.1.call-done = bf16[512,512]{0,1:T(8,128)(2,1)} async-done(((bf16[2048,512]{0,1:T(8,128)(2,1)}), bf16[512,512]{0,1:T(8,128)(2,1)}) %reduce-scatter.12.cloned.1.call-update) | async-done | bytes 524304 | tf_op jit(solution)/shard_map/reduce_scatter | solution.py:96
  313.6 1.1 constant_dynamic-update-slice_fusion.1
  314.6 44.5 %reduce-scatter.14.cloned.1.call-done = bf16[512,512]{0,1:T(8,128)(2,1)} async-done(((bf16[2048,512]{0,1:T(8,128)(2,1)}), bf16[512,512]{0,1:T(8,128)(2,1)}) %reduce-scatter.14.cloned.1.call-update) | async-done | bytes 524304 | tf_op jit(solution)/shard_map/reduce_scatter | solution.py:96
  359.1 1.1 constant_dynamic-update-slice_fusion
  360.2 2.4 copy.43
  (29 shorter events, 0.2 us)
Async XLA Ops:
  7.2 4.6 %copy-start.5 = (s32[16,4]{0,1:T(4,128)S(1)}, s32[16,4]{0,1:T(4,128)}, u32[]{:S(2)}) copy-start(s32[16,4]{0,1:T(4,128)} %param.9) | copy-start | bytes 772
  7.2 34.4 %all-gather.3.cloned.1.call-start = ((), (), s32[]{:S(2)}) async-start(), calls=%async_computation.5 | async-start | bytes 1310720 | tf_op jit(solution)/shard_map/all_gather | solution.py:71
  7.9 94.7 %reduce-scatter.6.cloned.1.call-start = ((), (), s32[]{:S(2)}) async-start(), calls=%async_computation.6 | async-start | bytes 1310720 | tf_op jit(solution)/shard_map/reduce_scatter | solution.py:96
  22.8 37.5 %copy-start.1 = (f32[256,256]{1,0:T(8,128)}, f32[256,256]{1,0:T(8,128)S(1)}, u32[]{:S(2)}) copy-start(f32[256,256]{1,0:T(8,128)S(1)} %reshape.46) | copy-start | bytes 786436
  41.6 88.2 %reduce-scatter.8.cloned.1.call-start = ((), (), s32[]{:S(2)}) async-start(), calls=%async_computation.7 | async-start | bytes 1310720 | tf_op jit(solution)/shard_map/reduce_scatter | solution.py:96
  64.2 22.4 %copy-start = (bf16[64,8192]{1,0:T(8,128)(2,1)S(1)}, bf16[64,8192]{1,0:T(8,128)(2,1)}, u32[]{:S(2)}) copy-start(bf16[64,8192]{1,0:T(8,128)(2,1)} %all-gather.3.cloned.1.call-done) | copy-start | bytes 3145732
  86.5 135.9 %all-reduce.3.cloned.1.call-start = ((), (), s32[]{:S(2)}) async-start(), calls=%async_computation.11 | async-start | bytes 262144
  100.4 3.1 copy-start.2
  102.7 165.4 %reduce-scatter.10.cloned.1.call-start = ((), (), s32[]{:S(2)}) async-start(), calls=%async_computation.8 | async-start | bytes 2621440 | tf_op jit(solution)/shard_map/reduce_scatter | solution.py:96
  103.2 210.3 %reduce-scatter.12.cloned.1.call-start = ((), (), s32[]{:S(2)}) async-start(), calls=%async_computation.9 | async-start | bytes 2621440 | tf_op jit(solution)/shard_map/reduce_scatter | solution.py:96
  129.8 229.3 %reduce-scatter.14.cloned.1.call-start = ((), (), s32[]{:S(2)}) async-start(), calls=%async_computation.10 | async-start | bytes 2621440 | tf_op jit(solution)/shard_map/reduce_scatter | solution.py:96
  133.8 22.4 %copy-start.6 = (u32[32]{0:T(128)S(1)}, u32[32]{0:T(128)}, u32[]{:S(2)}) copy-start(u32[32]{0:T(128)} %constant.64) | copy-start | bytes 388
  133.8 23.0 %copy-start.3 = (bf16[512,256]{0,1:T(8,128)(2,1)S(1)}, bf16[512,256]{0,1:T(8,128)(2,1)}, u32[]{:S(2)}) copy-start(bf16[512,256]{0,1:T(8,128)(2,1)} %reduce-scatter.6.cloned.1.call-done) | copy-start | bytes 786436
  133.8 23.0 %copy-start.4 = (bf16[512,256]{0,1:T(8,128)(2,1)S(1)}, bf16[512,256]{0,1:T(8,128)(2,1)}, u32[]{:S(2)}) copy-start(bf16[512,256]{0,1:T(8,128)(2,1)} %reduce-scatter.8.cloned.1.call-done) | copy-start | bytes 786436
Sparse Core Ops, SparseCore 0:
  9.9 29.3 all-gather.2
  41.7 27.4 reduce-scatter.5
  86.7 27.4 reduce-scatter.7
  119.5 102.9 all-reduce.2
  225.2 42.8 reduce-scatter.9
  270.4 43.1 reduce-scatter.11
  315.8 43.1 reduce-scatter.13

commit v2 on v1

--- a/solution.py
+++ b/solution.py
@@ -10,7 +10,7 @@
 BLOCK = 128
 LOW = 256
 GROUP = 8
-CHUNKS = (2, 2, 4, 4, 4)
+CHUNKS = (1, 3, 4)
 
 
 def dense_kernel(high_count, high_ref, low_ref, weight_ref, dense_ref):
@@ -68,9 +68,6 @@
     resident_blocks = range_width // BLOCK
     high_count = shard_width // LOW
 
-    all_rows = lax.all_gather(query_rows, "prange", axis=0, tiled=True)
-    all_candidates = lax.all_gather(candidates, "prange", axis=0, tiled=True)
-
     local_ids = term_ids - lax.axis_index("vocab") * shard_width
     high = local_ids // LOW
     low = (local_ids % LOW).astype(jnp.float32)
@@ -92,29 +89,31 @@
         part = lax.dot_general(
             impact, dense_query, (((0,), (1,)), ((), ())), preferred_element_type=jnp.float32
         ).astype(jnp.bfloat16)
-        codes, all_rows, part = lax.optimization_barrier((codes, all_rows, part))
+        codes, query_rows, candidates, part = lax.optimization_barrier(
+            (codes, query_rows, candidates, part)
+        )
         pieces.append(lax.psum_scatter(part, "vocab", scatter_dimension=0, tiled=True))
-        if len(pieces) >= 3:
-            codes, pieces[-3] = lax.optimization_barrier((codes, pieces[-3]))
-        if len(pieces) == 3:
-            scores = jnp.dot(all_rows, impact, preferred_element_type=jnp.float32)
-            scores = scores.reshape(-1, resident_blocks, BLOCK)
-            own = all_candidates - lax.axis_index("prange") * resident_blocks
-            chosen = own[:, :, None] == jnp.arange(resident_blocks, dtype=jnp.int32)
-            picked = jnp.sum(
-                jnp.where(chosen[:, :, :, None], scores[:, None, :, :], 0.0), axis=2
-            )
-            full_count, cands = candidates.shape
-            share_width = BLOCK // vocab_count
-            picked = picked.reshape(range_count, full_count * cands, vocab_count, share_width)
-            picked = picked.transpose(2, 0, 1, 3).reshape(
-                vocab_count * range_count, full_count * cands * share_width
-            )
-            codes, picked, pieces[0] = lax.optimization_barrier((codes, picked, pieces[0]))
-            summed = lax.psum_scatter(
-                picked, ("vocab", "prange"), scatter_dimension=0, tiled=True
-            )
-            rescored = summed.reshape(full_count, cands, share_width)
+
+    full_count, cands = candidates.shape
+    all_rows = lax.all_to_all(
+        jnp.broadcast_to(query_rows[None], (range_count, full_count, shard_width)),
+        "prange", split_axis=0, concat_axis=0, tiled=True,
+    ).reshape(range_count * full_count, shard_width)
+    all_candidates = lax.all_gather(candidates, "prange", axis=0, tiled=True)
+    scores = jnp.dot(all_rows, impact, preferred_element_type=jnp.float32)
+    scores = scores.reshape(-1, resident_blocks, BLOCK)
+    own = all_candidates - lax.axis_index("prange") * resident_blocks
+    chosen = own[:, :, None] == jnp.arange(resident_blocks, dtype=jnp.int32)
+    picked = jnp.sum(jnp.where(chosen[:, :, :, None], scores[:, None, :, :], 0.0), axis=2)
+    share_width = BLOCK // vocab_count
+    picked = picked.reshape(range_count, full_count * cands, vocab_count, share_width)
+    picked = picked.transpose(2, 0, 1, 3).reshape(
+        vocab_count * range_count, full_count * cands * share_width
+    )
+    arrived = lax.all_to_all(
+        picked, ("vocab", "prange"), split_axis=0, concat_axis=0, tiled=True
+    )
+    rescored = jnp.sum(arrived, axis=0).reshape(full_count, cands, share_width)
     first_scores = jnp.concatenate(pieces, axis=1)[None]
     return (first_scores, rescored)
 

time: 370 us -> 227 us (0.61)
  waiting for transfers between devices: 199 us -> 0.06 us
  local copies, waits for them, and re-layouts: 14 us -> 55.5 us
  blocking collectives: 9.52 us -> 23.8 us
  matrix products: 114 us -> 107 us
  starting transfers between devices: 0.68 us -> 5.2 us
    reduce_scatter x5 -> x3, waiting for transfers between devices: 132 us -> 0.01 us  [local(): lax.psum_scatter(part, 'vocab', scatter_dimension=0, tiled=True)]
    unnamed x8 -> x3, waiting for transfers between devices: 66.9 us -> 0.05 us
    another operation x0 -> x1, local copies, waits for them, and re-layouts: none -> 40.3 us
    all_to_all x0 -> x1, blocking collectives: none -> 15.2 us  [local(): lax.all_to_all(picked, ('vocab', 'prange'), split_axis=0, concat_axis=0,...]
    dot_general x5 -> x3, matrix products: 99.8 us -> 91.9 us  [local(): lax.dot_general(impact, dense_query, (((0,), (1,)), ((), ())), preferred_...]
    all_to_all x0 -> x1, starting transfers between devices: none -> 4.9 us  [local(): lax.all_to_all(jnp.broadcast_to(query_rows[None], (range_count, full_coun...]
    unnamed x22 -> x7, local copies, waits for them, and re-layouts: 6.79 us -> 8.42 us
    pallas_call x5 -> x3, Pallas kernels: 15.7 us -> 15.6 us  [densify(): pl.pallas_call(functools.partial(dense_kernel, high_count), grid=(groups...]
  transfers between devices with their start and end apart: 7 -> 4, of which waited for: 4 -> 0; matrix products, arithmetic and copies ran while one was open for 34% -> 60% of each run, Pallas kernels for 4% -> 6%
where the time goes in v2:
time: 227 us; the launch traced here: 226 us
  matrix products  107 us (47%)
  local copies, waits for them, and re-layouts  55.5 us (24%)
  blocking collectives  23.8 us (10%)
  Pallas kernels  15.6 us (7%)
  between operations  14 us (6%)
  starting transfers between devices  5.2 us (2%)
  other arithmetic  3.99 us (2%)
    dot_general x3, matrix products, local(): lax.dot_general(impact, dense_query, (((0,), (1,)), ((), ())), preferred_...  91.9 us
    another operation x1, local copies, waits for them, and re-layouts  40.3 us
    pallas_call x3, Pallas kernels, densify(): pl.pallas_call(functools.partial(dense_kernel, high_count), grid=(groups...  15.6 us
    dot_general x1, matrix products, local(): scores = jnp.dot(all_rows, impact, preferred_element_type=jnp.float32)  15.5 us
    all_to_all x1, blocking collectives, local(): lax.all_to_all(picked, ('vocab', 'prange'), split_axis=0, concat_axis=0,...  15.2 us
    all_gather x1, blocking collectives, local(): all_candidates = lax.all_gather(candidates, 'prange', axis=0, tiled=True)  8.58 us
    unnamed x7, local copies, waits for them, and re-layouts  8.42 us
    all_to_all x1, starting transfers between devices, local(): lax.all_to_all(jnp.broadcast_to(query_rows[None], (range_count, full_coun...  4.9 us
  transfers between devices with their start and end apart: 4, of which 0 were waited for; matrix products, arithmetic and copies ran while one was open for 60% of the time, Pallas kernels for 6%

profile of v2, /device:TPU:0, one launch (start us, length us, event | category | flops | bytes accessed | tf_op | source)
XLA Modules:
  0.0 225.6 jit_solution(14793285080813229999)
XLA Ops:
  7.2 0.0 reduce-scatter.4.cloned.1.call-start
  7.2 1.3 fusion.2
  8.5 0.3 copy.41
  8.8 0.3 copy.42
  9.2 1.1 copy.43
  10.3 0.7 slice.50
  11.0 0.3 reshape.56
  11.3 0.3 reshape.57
  11.7 0.3 reshape.58
  12.0 0.1 copy.44
  12.1 0.1 slice.37.high_ref
  12.2 0.1 copy.45
  12.3 0.1 slice.39.low_ref
  12.4 0.1 copy.46
  12.5 0.1 slice.41.weight_ref
  12.6 2.0 shard_map.68
  14.6 16.2 %fusion.1 = bf16[2048,256]{0,1:T(8,128)(2,1)} fusion(bf16[256,8192]{1,0:T(8,128)(2,1)S(1)} %shard_map.68, bf16[8192,2048]{1,0:T(8,128)(2,1)} %param.7), kind=kOutput, calls=%fused_computation.4 | convolution fusion | flops 8590458880 | bytes 38797312 | tf_op jit(solution)/shard_map/dot_general | solution.py:89
  30.8 0.0 reduce-scatter.4.cloned.1.call-update
  30.8 0.0 reduce-scatter.6.cloned.1.call-start
  30.9 5.8 %shard_map.69 = bf16[768,8192]{1,0:T(8,128)(2,1)S(1)} custom-call(f32[96,256]{1,0:T(8,128)S(1)} %slice.42.high_ref, f32[96,256]{1,0:T(8,128)S(1)} %slice.43.low_ref, f32[96,256]{1,0:T(8,128)S(1)} %slice.44.weight_ref), custom_call_target="tpu_custom_call" | custom-call | flops 3221225472 | bytes 12582912 | tf_op jit(solution)/shard_map/pallas_call | solution.py:48
  36.8 31.1 %fusion = bf16[2048,768]{0,1:T(8,128)(2,1)} fusion(bf16[768,8192]{1,0:T(8,128)(2,1)S(1)} %shard_map.69, bf16[8192,2048]{1,0:T(8,128)(2,1)} %param.7), kind=kOutput, calls=%fused_computation.2 | convolution fusion | flops 25771376640 | bytes 49283072 | tf_op jit(solution)/shard_map/dot_general | solution.py:89
  67.8 0.0 reduce-scatter.6.cloned.1.call-update
  67.9 0.2 reduce-scatter.8.cloned.1.call-start
  68.1 7.8 %shard_map.70 = bf16[1024,8192]{1,0:T(8,128)(2,1)S(1)} custom-call(f32[128,256]{1,0:T(8,128)S(1)} %slice.45.high_ref, f32[128,256]{1,0:T(8,128)S(1)} %slice.46.low_ref, f32[128,256]{1,0:T(8,128)S(1)} %slice.47.weight_ref), custom_call_target="tpu_custom_call" | custom-call | flops 4294967296 | bytes 16777216 | tf_op jit(solution)/shard_map/pallas_call | solution.py:48
  75.9 0.0 copy-start
  76.0 6.0 %copy-done = bf16[1024,8192]{1,0:T(8,128)(2,1)} copy-done((bf16[1024,8192]{1,0:T(8,128)(2,1)}, bf16[1024,8192]{1,0:T(8,128)(2,1)S(1)}, u32[]{:S(2)}) %copy-start) | copy-done | bytes 16777240
  82.0 0.0 copy-start.1
  82.0 44.6 %convert_bitcast_fusion = bf16[2048,1024]{0,1:T(8,128)(2,1)} fusion(bf16[1024,8192]{1,0:T(8,128)(2,1)} %copy-done, bf16[8192,2048]{1,0:T(8,128)(2,1)} %param.7), kind=kOutput, calls=%fused_computation | convolution fusion | flops 34361835520 | bytes 54525952 | tf_op jit(solution)/shard_map/dot_general | solution.py:89
  126.6 0.0 reduce-scatter.8.cloned.1.call-update
  126.6 0.0 copy-done.1
  126.6 1.0 broadcast_in_dim.37
  127.7 4.9 %all-to-all-start = ((bf16[4,16,8192]{2,1,0:T(8,128)(2,1)}), bf16[4,16,8192]{2,1,0:T(8,128)(2,1)S(1)}, u32[]{:S(2)}, u32[]{:S(2)}) async-start(bf16[4,16,8192]{2,1,0:T(8,128)(2,1)} %broadcast_in_dim.37), calls=%async_computation.3 | async-start | bytes 2097152 | tf_op jit(solution)/shard_map/all_to_all | solution.py:98
  132.6 0.0 copy-start.2
  132.6 40.3 %copy.55 = bf16[2048,8192]{1,0:T(8,128)(2,1)} copy(bf16[2048,8192]{0,1:T(8,128)(2,1)} %bitcast.29) | data formatting | bytes 67108864 | tf_op jit(solution)/shard_map/reshape.24
  172.9 0.0 copy-done.2
  172.9 8.6 %all-gather = s32[4,16,4]{1,2,0:T(4,128)S(1)} all-gather(s32[1,16,4]{1,2,0:T(4,128)S(1)} %bitcast.35), channel_id=1, replica_groups=mesh['vocab'=4,'prange'=4,'query'=2] {'prange'}, dimensions={0}, use_global_device_ids=true | all-gather | bytes 1280 | tf_op jit(solution)/shard_map/all_gather | solution.py:102
  181.5 0.1 copy.54
  181.6 0.1 iota_compare_fusion
  181.8 0.0 all-to-all-done
  181.8 15.5 %fusion.8 = f32[64,16,128]{2,0,1:T(8,128)S(1)} fusion(bf16[64,8192,1]{1,0,2:T(8,128)(2,1)S(1)} %bitcast.30, bf16[16,128,8192]{2,1,0:T(8,128)(2,1)} %bitcast.28), kind=kOutput, calls=%fused_computation.25 | convolution fusion | flops 2147483648 | bytes 35127296 | tf_op jit(solution)/shard_map/dot_general | solution.py:103
  197.2 0.3 copy.50
  197.6 0.9 select_reduce_fusion
  198.4 0.3 reshape.61
  198.8 0.3 all_to_all.12
  199.0 15.2 %all_to_all.15 = f32[16,1,2048]{2,1,0:T(1,128)S(1)} all-to-all(f32[16,1,2048]{2,1,0:T(1,128)S(1)} %all_to_all.12), channel_id=1, replica_groups=mesh['vocab'=4,'prange'=4,'query'=2] {'vocab','prange'}, dimensions={0} | all-to-all | bytes 262144 | tf_op jit(solution)/shard_map/all_to_all | solution.py:113
  214.2 0.1 reduce_sum.19
  214.3 0.7 reshape.62
  215.0 0.0 reduce-scatter.4.cloned.1.call-done
  215.0 0.0 reduce-scatter.6.cloned.1.call-done
  215.0 0.0 reduce-scatter.8.cloned.1.call-done
  215.0 1.6 maximum_bitcast_fusion
  216.7 2.4 %copy.53 = bf16[1,512,2048]{2,1,0:T(8,128)(2,1)} copy(bf16[1,512,2048]{1,2,0:T(8,128)(2,1)S(1)} %maximum_bitcast_fusion) | data formatting | bytes 4194304
  (11 shorter events, 0.1 us)
Async XLA Ops:
  7.2 207.9 %reduce-scatter.4.cloned.1.call-start = ((), (), s32[]{:S(2)}) async-start(), calls=%async_computation.5 | async-start | bytes 1310720 | tf_op jit(solution)/shard_map/reduce_scatter | solution.py:95
  30.8 184.2 %reduce-scatter.6.cloned.1.call-start = ((), (), s32[]{:S(2)}) async-start(), calls=%async_computation.6 | async-start | bytes 3932160 | tf_op jit(solution)/shard_map/reduce_scatter | solution.py:95
  67.9 147.2 %reduce-scatter.8.cloned.1.call-start = ((), (), s32[]{:S(2)}) async-start(), calls=%async_computation.7 | async-start | bytes 5242880 | tf_op jit(solution)/shard_map/reduce_scatter | solution.py:95
  75.9 6.0 %copy-start = (bf16[1024,8192]{1,0:T(8,128)(2,1)}, bf16[1024,8192]{1,0:T(8,128)(2,1)S(1)}, u32[]{:S(2)}) copy-start(bf16[1024,8192]{1,0:T(8,128)(2,1)S(1)} %shard_map.70) | copy-start | bytes 50331652
  82.0 44.7 %copy-start.1 = (bf16[16,8192]{1,0:T(8,128)(2,1)S(1)}, bf16[16,8192]{1,0:T(8,128)(2,1)}, u32[]{:S(2)}) copy-start(bf16[16,8192]{1,0:T(8,128)(2,1)} %param.8) | copy-start | bytes 786436
  127.7 54.1 %all-to-all-start = ((bf16[4,16,8192]{2,1,0:T(8,128)(2,1)}), bf16[4,16,8192]{2,1,0:T(8,128)(2,1)S(1)}, u32[]{:S(2)}, u32[]{:S(2)}) async-start(bf16[4,16,8192]{2,1,0:T(8,128)(2,1)} %broadcast_in_dim.37), calls=%async_computation.3 | async-start | bytes 2097152 | tf_op jit(solution)/shard_map/all_to_all | solution.py:98
  132.6 40.3 %copy-start.2 = (s32[16,4]{0,1:T(4,128)S(1)}, s32[16,4]{0,1:T(4,128)}, u32[]{:S(2)}) copy-start(s32[16,4]{0,1:T(4,128)} %param.9) | copy-start | bytes 772
Sparse Core Ops, SparseCore 0:
  30.9 29.8 reduce-scatter.3
  68.0 62.9 reduce-scatter.5
  133.4 78.0 reduce-scatter.7
